TPU v7x, 32 devices: a whole 2x2x4 slice. The times are simulated.
32 devices in a mesh: groups: 2 (over y), seq: 8 (over z, core), dp: 2 (over x).
Axes of the slice: x: 2, y: 2, z: 4, core: 2. Of those that a mesh axis runs over, the one named last changes fastest.
Arguments:
- tokens: bfloat16 [4, 1024, 1024], P(('groups', 'dp'), 'seq'), parts along dimension 0, may hold values from -6 to 6
- w_query: bfloat16 [1024, 1024], replicated, may hold values from -0.1875 to 0.1875
- w_key: bfloat16 [1024, 1024], replicated, may hold values from -0.1875 to 0.1875
- w_value: bfloat16 [1024, 1024], replicated, may hold values from -0.1875 to 0.1875
- w_output: bfloat16 [1024, 1024], replicated, may hold values from -0.1875 to 0.1875
- out_cotangent: bfloat16 [4, 1024, 1024], P(('groups', 'dp'), 'seq'), parts along dimension 0, may hold values from -6 to 6
Outputs:
- attended: bfloat16 [4, 1024, 1024], P(('groups', 'dp'), 'seq'), parts along dimension 0
- d_tokens: bfloat16 [4, 1024, 1024], P(('groups', 'dp'), 'seq'), parts along dimension 0
- weight_grads: float32 [2048, 4096], P(('groups', 'seq', 'dp')), parts along dimension 0
There are 2 independent parts, one for each index of `groups`. A program takes and returns all parts, laid end to end along the dimension named above; an argument that names none is the same for every part. Nothing has to cross between parts.
All inputs are finite; a program needn't handle non-finite values.
Results may differ from a plain program's by a relative error of at most 0.008.
Values sent between devices are 32-bit elements; how exact they have to be, the bound alone decides.
A program may use at most 128 MiB of HBM per device.

v0:
```python
import math

import jax
import jax.numpy as jnp
from jax import lax
from jax.sharding import PartitionSpec as P

H = 8


EPSILON = 1e-05


def entering(value, axis, combine, identity, reverse):
    devices, place = (lax.axis_size(axis), lax.axis_index(axis))
    everything = lax.all_gather(value, axis)
    start = jnp.broadcast_to(jnp.asarray(identity, value.dtype), value.shape)

    def hop(k, before):
        at = devices - 1 - k if reverse else k
        reached = at > place if reverse else at < place
        new = combine(before, everything[at])
        return jnp.where(reached, new, before)

    return lax.fori_loop(0, devices, hop, start)


def causal_mask(row_count):
    rows = lax.broadcasted_iota(jnp.int32, (row_count, row_count), 0)
    cols = lax.broadcasted_iota(jnp.int32, (row_count, row_count), 1)
    return rows >= cols


def add_states(earlier, later_part):
    return earlier + later_part


def local(tokens, w_query, w_key, w_value, w_output, out_cotangent):
    clip_count, row_count, model_width = tokens.shape
    head_count = H
    head_size = model_width // head_count
    flattened = tokens.reshape(clip_count * row_count, model_width)

    def project(weight):
        product = jnp.dot(flattened, weight, preferred_element_type=jnp.float32).astype(
            jnp.bfloat16
        )
        return product.reshape(clip_count, row_count, head_count, head_size)

    queries = project(w_query)
    key_rows = project(w_key)
    value_rows = project(w_value)
    own_state = jnp.einsum(
        "cshd,cshe->chde", key_rows, value_rows, preferred_element_type=jnp.float32
    )
    carried = entering(own_state, "seq", add_states, jnp.zeros_like(own_state), False)
    carried = carried.astype(jnp.bfloat16)
    causal = causal_mask(row_count)
    scores = jnp.einsum("cthd,cshd->chts", queries, key_rows, preferred_element_type=jnp.float32)
    attn_weights = jnp.where(causal, scores, 0.0).astype(jnp.bfloat16)
    mixed = jnp.einsum(
        "chts,cshd->cthd", attn_weights, value_rows, preferred_element_type=jnp.float32
    )
    mixed = mixed + jnp.einsum(
        "cthd,chde->cthe", queries, carried, preferred_element_type=jnp.float32
    )
    mixed = mixed.reshape(clip_count, row_count, model_width)
    scale_rows = jnp.sqrt(jnp.mean(mixed * mixed, axis=-1, keepdims=True) + EPSILON)
    normed = mixed / scale_rows
    normed_flat = normed.astype(jnp.bfloat16).reshape(-1, model_width)
    attended = jnp.dot(normed_flat, w_output, preferred_element_type=jnp.float32).astype(
        jnp.bfloat16
    )
    attended = attended.reshape(clip_count, row_count, model_width)
    cot_flat = out_cotangent.reshape(-1, model_width)
    back_norm = jnp.einsum("ne,de->nd", cot_flat, w_output, preferred_element_type=jnp.float32)
    back_norm = back_norm.reshape(clip_count, row_count, model_width)
    d_mixed = (
        (back_norm - normed * jnp.mean(back_norm * normed, axis=-1, keepdims=True)) / scale_rows
    ).astype(jnp.bfloat16)
    d_heads = d_mixed.reshape(clip_count, row_count, head_count, head_size)
    own_back = jnp.einsum("cthd,cthe->chde", queries, d_heads, preferred_element_type=jnp.float32)
    later = entering(own_back, "seq", add_states, jnp.zeros_like(own_back), True)
    later = later.astype(jnp.bfloat16)
    back_scores = jnp.einsum(
        "cthe,cshe->chts", d_heads, value_rows, preferred_element_type=jnp.float32
    )
    back_scores = jnp.where(causal, back_scores, 0.0).astype(jnp.bfloat16)
    d_query = jnp.einsum(
        "chts,cshd->cthd", back_scores, key_rows, preferred_element_type=jnp.float32
    )
    d_query = d_query + jnp.einsum(
        "cthe,chde->cthd", d_heads, carried, preferred_element_type=jnp.float32
    )
    d_key = jnp.einsum("chts,cthd->cshd", back_scores, queries, preferred_element_type=jnp.float32)
    d_key = d_key + jnp.einsum(
        "cshe,chde->cshd", value_rows, later, preferred_element_type=jnp.float32
    )
    d_value = jnp.einsum(
        "chts,cthe->cshe", attn_weights, d_heads, preferred_element_type=jnp.float32
    )
    d_value = d_value + jnp.einsum(
        "cshd,chde->cshe", key_rows, later, preferred_element_type=jnp.float32
    )
    d_query = d_query.astype(jnp.bfloat16).reshape(-1, model_width)
    d_key = d_key.astype(jnp.bfloat16).reshape(-1, model_width)
    d_value = d_value.astype(jnp.bfloat16).reshape(-1, model_width)
    d_tokens = jnp.einsum("nd,ed->ne", d_query, w_query, preferred_element_type=jnp.float32)
    d_tokens = d_tokens + jnp.einsum("nd,ed->ne", d_key, w_key, preferred_element_type=jnp.float32)
    d_tokens = d_tokens + jnp.einsum(
        "nd,ed->ne", d_value, w_value, preferred_element_type=jnp.float32
    )
    d_tokens = d_tokens.astype(jnp.bfloat16).reshape(clip_count, row_count, model_width)
    joined = jnp.concatenate([d_query, d_key, d_value], axis=1)
    summed = lax.psum_scatter(
        jnp.concatenate(
            [
                jnp.einsum("nd,ne->de", flattened, joined, preferred_element_type=jnp.float32),
                jnp.einsum("nd,ne->de", normed_flat, cot_flat, preferred_element_type=jnp.float32),
            ],
            axis=1,
        ),
        ("seq", "dp"),
        scatter_dimension=0,
        tiled=True,
    )
    token_total = clip_count * lax.axis_size("dp") * row_count * lax.axis_size("seq")
    weight_grads = summed * (1.0 / math.sqrt(token_total))
    return (attended, d_tokens, weight_grads)


def solution(mesh):
    return jax.shard_map(
        local,
        mesh=mesh,
        in_specs=(
            P(("groups", "dp"), "seq", None),
            P(),
            P(),
            P(),
            P(),
            P(("groups", "dp"), "seq", None),
        ),
        out_specs=(
            P(("groups", "dp"), "seq", None),
            P(("groups", "dp"), "seq", None),
            P(("groups", "seq", "dp"), None),
        ),
        check_vma=False,
    )
```

profile of v0, /device:TPU:0, one launch (start us, length us, event | category | flops | bytes accessed | tf_op | source)
XLA Modules:
  0.0 358.0 jit_solution(14721868097175616498)
XLA Ops:
  7.2 2.3 fusion.7
  11.6 2.7 convolution_convert_fusion.2
  15.5 1.4 fusion
  18.7 42.8 %all-gather.5.cloned.1.call-done = f32[64,128,128]{2,1,0:T(8,128)} async-done(((f32[8,128,128]{2,1,0:T(8,128)}), f32[64,128,128]{2,1,0:T(8,128)}) %all-gather.5.cloned.1.call-update) | async-done | bytes 4194320 | tf_op jit(solution)/shard_map/all_gather | solution.py:16
  61.5 10.0 %while.30 = (s32[]{:T(128)}, f32[1,8,128,128]{3,2,1,0:T(8,128)S(1)}, s32[]{:T(128)}, f32[8,1,8,128,128]{4,3,2,1,0:T(8,128)}, s32[]{:T(128)}, /*index=5*/s32[]{:T(128)}) while((s32[]{:T(128)}, f32[1,8,128,128]{3,2,1,0:T(8,128)S(1)}, s32[]{:T(128)}, f32[8,1,8,128,128]{4,3,2,1,0:T(8,128)}, s32[]{:T(128)}, /*index=5*/s32[]{:T(128)}) %tuple.92), condition=%wide.region_1.2_spmd.clone, body=%wide.region_0.1_spmd.clone.sunk | while | flops 393220 | bytes 1572965 | solution.py:25
  71.5 1.5 fusion.15
  74.0 2.1 multiply_reduce_fusion
  76.5 2.1 fusion.51
  79.9 1.4 fusion.1
  81.3 1.2 fusion.48
  85.6 2.8 fusion.26
  88.4 36.3 %all-gather.7.cloned.1.call-done = f32[64,128,128]{2,1,0:T(8,128)} async-done(((f32[8,128,128]{2,1,0:T(8,128)}), f32[64,128,128]{2,1,0:T(8,128)}) %all-gather.7.cloned.1.call-update) | async-done | bytes 4194320 | tf_op jit(solution)/shard_map/all_gather | solution.py:16
  124.7 10.1 %while.31 = (s32[]{:T(128)}, f32[1,8,128,128]{3,2,1,0:T(8,128)S(1)}, s32[]{:T(128)}, f32[8,1,8,128,128]{4,3,2,1,0:T(8,128)}, s32[]{:T(128)}, /*index=5*/s32[]{:T(128)}, s32[]{:T(128)}, s32[]{:T(128)}) while((s32[]{:T(128)}, f32[1,8,128,128]{3,2,1,0:T(8,128)S(1)}, s32[]{:T(128)}, f32[8,1,8,128,128]{4,3,2,1,0:T(8,128)}, s32[]{:T(128)}, ...), condition=%wide.region_5.6_spmd.clone, body=%wide.region_4.5_spmd.clone.sunk | while | flops 393224 | bytes 1573027 | solution.py:25
  124.7 1.3 add_select_fusion.5
  134.8 1.4 fusion.3
  136.2 1.5 fusion.4
  137.7 1.8 convolution_bitcast_fusion
  139.9 7.1 %pad_maximum_fusion = f32[1024,4096]{0,1:T(8,128)} fusion(f32[1024,1024]{0,1:T(8,128)S(1)} %copy-done.1, f32[1024,3072]{0,1:T(8,128)S(1)} %convolution_bitcast_fusion), kind=kLoop, calls=%fused_computation.2 | loop fusion | flops 4194304 | bytes 33554432 | tf_op jit(solution)/shard_map/concatenate | solution.py:116
  147.1 17.5 %copy.55 = f32[1024,4096]{1,0:T(8,128)} copy(f32[1024,4096]{0,1:T(8,128)} %pad_maximum_fusion) | data formatting | bytes 33554432
  170.6 1.6 fusion.6
  172.2 169.9 %reduce-scatter.4.cloned.1.call-done = f32[64,4096]{1,0:T(8,128)} async-done(((f32[1024,4096]{1,0:T(8,128)}), f32[64,4096]{1,0:T(8,128)}) %reduce-scatter.4.cloned.1.call-update) | async-done | bytes 1048592
  342.0 3.2 copy.56
  345.2 3.1 broadcast_multiply_fusion
  348.3 3.1 copy.52
  (90 shorter events, 35.5 us)
Async XLA Ops:
  7.2 66.9 %copy-start = (bf16[1024,1024]{1,0:T(8,128)(2,1)S(1)}, bf16[1024,1024]{1,0:T(8,128)(2,1)}, u32[]{:S(2)}) copy-start(bf16[1024,1024]{1,0:T(8,128)(2,1)} %param.14) | copy-start | bytes 6291460
  7.2 2.3 copy-start.7
  7.2 54.3 %all-gather.5.cloned.1.call-start = ((), (), s32[]{:S(2)}) async-start(), calls=%async_computation.1 | async-start | bytes 4718592 | tf_op jit(solution)/shard_map/all_gather | solution.py:16
  7.2 2.5 copy-start.4
  9.7 7.2 %copy-start.8 = (bf16[16,8,8,128]{3,2,1,0:T(8,128)(2,1)}, bf16[16,8,8,128]{3,2,1,0:T(8,128)(2,1)S(1)}, u32[]{:S(2)}) copy-start(bf16[16,8,8,128]{3,2,1,0:T(8,128)(2,1)S(1)} %fusion.7) | copy-start | bytes 786436
  10.2 1.4 copy-start.17
  11.5 113.2 %all-gather.7.cloned.1.call-start = ((), (), s32[]{:S(2)}) async-start(), calls=%async_computation.2 | async-start | bytes 4718592 | tf_op jit(solution)/shard_map/all_gather | solution.py:16
  15.5 46.0 %copy-start.10 = (bf16[128,1024]{0,1:T(8,128)(2,1)}, bf16[128,1024]{0,1:T(8,128)(2,1)S(1)}, u32[]{:S(2)}) copy-start(bf16[128,1024]{0,1:T(8,128)(2,1)S(1)} %copy.57) | copy-start | bytes 786436
  73.0 3.1 copy-start.6
  74.0 2.1 copy-start.19
  76.5 2.2 copy-start.12
  78.7 263.3 %reduce-scatter.4.cloned.1.call-start = ((), (), s32[]{:S(2)}) async-start(), calls=%async_computation.3 | async-start | bytes 17825792
  78.7 3.8 %copy-start.11 = (bf16[128,1024]{0,1:T(8,128)(2,1)S(1)}, bf16[128,1024]{0,1:T(8,128)(2,1)}, u32[]{:S(2)}) copy-start(bf16[128,1024]{0,1:T(8,128)(2,1)} %copy-done.10) | copy-start | bytes 786436
  78.7 4.9 %copy-start.13 = (bf16[128,1024]{0,1:T(8,128)(2,1)S(1)}, bf16[128,1024]{0,1:T(8,128)(2,1)}, u32[]{:S(2)}) copy-start(bf16[128,1024]{0,1:T(8,128)(2,1)} %copy-done.12) | copy-start | bytes 786436
  78.8 4.9 %copy-start.22 = (bf16[8,128,128]{2,1,0:T(8,128)(2,1)S(1)}, bf16[8,128,128]{2,1,0:T(8,128)(2,1)}, u32[]{:S(2)}) copy-start(bf16[8,128,128]{2,1,0:T(8,128)(2,1)} %copy-done.21) | copy-start | bytes 786436
  82.6 3.1 copy-start.23
  124.7 10.1 %copy-start.9 = (bf16[16,8,8,128]{3,2,1,0:T(8,128)(2,1)S(1)}, bf16[16,8,8,128]{3,2,1,0:T(8,128)(2,1)}, u32[]{:S(2)}) copy-start(bf16[16,8,8,128]{3,2,1,0:T(8,128)(2,1)} %copy-done.8) | copy-start | bytes 786436
  134.8 3.0 copy-start.14
  136.2 1.6 copy-start.15
  137.7 2.2 copy-start.1
  165.6 1.7 copy-start.3
  167.3 1.6 copy-start.5
  167.3 1.7 copy-start.16
  169.0 1.6 copy-start.2
  (3 other events, 2.9 us)
Sparse Core Ops, SparseCore 0:
  11.7 49.8 all-gather.4
  78.8 45.8 all-gather.6
  164.7 177.2 reduce-scatter.3
where the time goes:
time: 360 us; the launch traced here: 358 us
  waiting for transfers between devices  249 us (69%)
  matrix products  32.2 us (9%)
  other arithmetic  31.3 us (9%)
  local copies, waits for them, and re-layouts  30.9 us (9%)
  between operations  14.1 us (4%)
    unnamed x4, waiting for transfers between devices  170 us
    all_gather x2, waiting for transfers between devices, entering(): everything = lax.all_gather(value, axis)  79.1 us
    unnamed x52, local copies, waits for them, and re-layouts  28.4 us
    select_n x16, other arithmetic, hop(): return jnp.where(reached, new, before)  19.7 us
  transfers between devices with their start and end apart: 3, of which 3 were waited for; matrix products, arithmetic and copies ran while one was open for 6% of the time, Pallas kernels for 0%

commit v1 on v0

v1 whole, which is shorter than its diff:
```python
import functools
import math

import jax
import jax.numpy as jnp
from jax import lax
from jax.experimental import pallas as pl
from jax.experimental.pallas import tpu as pltpu
from jax.sharding import PartitionSpec as P

H = 8
EPSILON = 1e-05
MESH = pl.DeviceIdType.MESH
F32, BF16 = jnp.float32, jnp.bfloat16
COLUMN_BLOCK = (3, 0, 1, 2)


def mm(a, b, ca, cb):
    return lax.dot_general(a, b, (((ca,), (cb,)), ((), ())), preferred_element_type=F32)


def kernel(
    n_seq, m,
    tok_ref, cot_ref, wq_hbm, wk_hbm, wv_hbm, wo_hbm,
    att_ref, dtok_ref, wg_ref,
    wq, wk, wv, wo,
    q_s, k_s, v_s, attn_s, mixed_s, back_s, carried_s, later_s, dm_s, nb_s, dqkv_s,
    gbuf, xt, xland, lhs, part, inb, sown, spart, crecv, csend,
    w_sem, g_send, g_fwd, g_recv, x_send, x_recv, e_send, e_recv,
    c_send, c_recv, p_send, p_recv, r_send, r_recv,
):
    t_rows, width = tok_ref.shape
    dh = width // H
    half = H // 2
    n_z = n_seq // 2
    rows = wg_ref.shape[0]
    members = 2 * m
    s, d = lax.axis_index("seq"), lax.axis_index("dp")
    z, c = lax.div(s, 2), lax.rem(s, 2)
    me = c * m + d
    up, down = z < n_z - 1, z > 0
    partner = {"seq": 2 * z + 1 - c, "dp": d}
    above = {"seq": jnp.minimum(s + 2, n_seq - 2 + c), "dp": d}
    below = {"seq": jnp.maximum(s - 2, c), "dp": d}
    pending = []

    def rcopy(src, dst, ss, rs, dev):
        return pltpu.make_async_remote_copy(
            src_ref=src, dst_ref=dst, send_sem=ss, recv_sem=rs,
            device_id=dev, device_id_type=MESH,
        )

    def arrived(ref, sem):
        rcopy(ref, ref, w_sem.at[0], sem, partner).wait_recv()

    loads = [
        pltpu.make_async_copy(src, dst, w_sem.at[i])
        for i, (src, dst) in enumerate(
            ((wk_hbm, wk), (wv_hbm, wv), (wq_hbm, wq), (wo_hbm, wo))
        )
    ]
    for load in loads:
        load.start()

    def member(rel):
        t = lax.rem(me + rel, members)
        return t, lax.div(t, m), lax.rem(t, m)

    barrier = pltpu.get_barrier_semaphore()
    for rel in range(1, members):
        _, tc, td = member(rel)
        pl.semaphore_signal(
            barrier, inc=1, device_id={"seq": 2 * z + tc, "dp": td}, device_id_type=MESH
        )

    @pl.when(up)
    def _():
        pl.semaphore_signal(barrier, inc=1, device_id=above, device_id_type=MESH)

    @pl.when(down)
    def _():
        pl.semaphore_signal(barrier, inc=1, device_id=below, device_id_type=MESH)

    pl.semaphore_wait(
        barrier, members - 1 + jnp.where(up, 1, 0) + jnp.where(down, 1, 0)
    )

    def gather_start(k, value):
        gbuf[k, me] = value
        own = gbuf.at[k, me]
        first = rcopy(own, own, g_send.at[k, 0], g_recv.at[k, me], partner)
        first.start()
        pending.append((None, first))
        for j in range(1, m):
            to = {"seq": s, "dp": lax.rem(d + j, m)}
            copy = rcopy(own, own, g_send.at[k, j], g_recv.at[k, me], to)
            copy.start()
            pending.append((None, copy))

    def gather_forward(k):
        for j in range(1, m):
            slot = c * m + lax.rem(d + m - j, m)
            ref = gbuf.at[k, slot]
            arrived(ref, g_recv.at[k, slot])
            copy = rcopy(ref, ref, g_fwd.at[k, j], g_recv.at[k, slot], partner)
            copy.start()
            pending.append((None, copy))

    def gather_finish(k):
        for j in range(m):
            slot = (1 - c) * m + j
            arrived(gbuf.at[k, slot], g_recv.at[k, slot])

    def columns_start(kind, value):
        xt[kind] = value.T.reshape(n_z, 2, m, rows, t_rows)
        xland[kind, me] = xt[kind, :, c, d]
        for rel in range(1, members):
            t, tc, td = member(rel)
            copy = rcopy(
                xt.at[kind, :, tc, td], xland.at[kind, me], x_send.at[kind, rel],
                x_recv.at[kind, me], {"seq": 2 * z + tc, "dp": td},
            )
            copy.start()
            pending.append((None, copy))

    def columns_finish(kind):
        for rel in range(1, members):
            t, _, _ = member(rel)
            arrived(xland.at[kind, t], x_recv.at[kind, t])
        for j in range(members):
            lhs[kind, :, j * t_rows:(j + 1) * t_rows] = (
                xland[kind, j].reshape(n_z * rows, t_rows).astype(BF16)
            )

    def exchange_start(way):
        copy = rcopy(sown.at[way], spart.at[way], e_send.at[way], e_recv.at[way], partner)
        copy.start()
        pending.append((None, copy))

    def chain(way):
        has_in, has_out, to = (down, up, above) if way == 0 else (up, down, below)
        arrived(spart.at[way], e_recv.at[way])

        @pl.when(jnp.logical_not(has_in))
        def _():
            crecv[way] = jnp.zeros(crecv.shape[1:], F32)

        for j in range(half):
            h = c * half + j
            ref = crecv.at[way, h]
            side = rcopy(ref, ref, p_send.at[way, j], p_recv.at[way, j], partner)
            ahead = rcopy(csend.at[way, j], ref, c_send.at[way, j], c_recv.at[way, j], to)

            @pl.when(has_in)
            def _():
                arrived(ref, c_recv.at[way, j])

            @pl.when(has_out)
            def _():
                csend[way, j] = crecv[way, h] + (sown[way, h] + spart[way, h])
                ahead.start()

            @pl.when(has_in)
            def _():
                side.start()

            pending.append((has_in, side))
            pending.append((has_out, ahead))

    def chain_finish(way, out):
        has_in = down if way == 0 else up
        for j in range(half):
            @pl.when(has_in)
            def _():
                arrived(crecv.at[way, (1 - c) * half + j], p_recv.at[way, j])

        takes = c == 1 - way
        for h in range(H):
            out[h] = jnp.where(
                takes, crecv[way, h] + spart[way, h], crecv[way, h]
            ).astype(BF16)

    def block_up(k, zp):
        ref = part.at[k, zp]
        return rcopy(ref, inb.at[k, zp], r_send.at[k, zp], r_recv.at[k, zp], above)

    def block_down(k, zp):
        slot = jnp.where(zp == z - 1, n_z, zp)
        return rcopy(
            part.at[k, zp], inb.at[k, slot], r_send.at[k, zp], r_recv.at[k, slot], below
        )

    def partial(k):
        right = gbuf[k].reshape(members * t_rows, width).astype(BF16)
        left = lhs[1 if k == 0 else 0]
        part[k] = mm(left, right, 1, 0).reshape(n_z, rows, width)

        @pl.when(z == 0)
        def _():
            for zp in reversed(range(1, n_z)):
                block_up(k, zp).start()

        @pl.when(z == n_z - 1)
        def _():
            for zp in range(n_z - 1):
                block_down(k, zp).start()

    def pass_on(k):
        for step in range(n_z - 1):
            high, low = n_z - 1 - step, step

            @pl.when((z > 0) & (z < high))
            def _():
                arrived(inb.at[k, high], r_recv.at[k, high])
                part[k, high] = part[k, high] + inb[k, high]
                block_up(k, high).start()

            @pl.when((z < n_z - 1) & (z > low))
            def _():
                arrived(inb.at[k, low], r_recv.at[k, low])
                part[k, low] = part[k, low] + inb[k, low]
                block_down(k, low).start()

    token_total = t_rows * n_seq * m

    def finish(k):
        @pl.when(down)
        def _():
            arrived(inb.at[k, z], r_recv.at[k, z])
            part[k, z] = part[k, z] + inb[k, z]

        @pl.when(up)
        def _():
            arrived(inb.at[k, n_z], r_recv.at[k, n_z])
            part[k, z] = part[k, z] + inb[k, n_z]

        at = COLUMN_BLOCK[k] * width
        wg_ref[:, at:at + width] = part[k, z] * (1.0 / math.sqrt(token_total))

    def head(h):
        return slice(h * dh, (h + 1) * dh)

    loads[0].wait()
    k_s[...] = mm(tok_ref[...], wk[...], 1, 0).astype(BF16)
    loads[1].wait()
    v_s[...] = mm(tok_ref[...], wv[...], 1, 0).astype(BF16)
    for h in range(H):
        sown[0, h] = mm(k_s[:, head(h)], v_s[:, head(h)], 0, 0)
    exchange_start(0)
    gather_start(0, cot_ref[...].astype(F32))
    loads[2].wait()
    q_s[...] = mm(tok_ref[...], wq[...], 1, 0).astype(BF16)
    chain(0)
    columns_start(0, tok_ref[...].astype(F32))
    loads[3].wait()
    back_s[...] = mm(cot_ref[...], wo[...], 1, 1)
    causal = lax.broadcasted_iota(jnp.int32, (t_rows, t_rows), 0) >= (
        lax.broadcasted_iota(jnp.int32, (t_rows, t_rows), 1)
    )
    for h in range(H):
        scores = mm(q_s[:, head(h)], k_s[:, head(h)], 1, 1)
        weights = jnp.where(causal, scores, 0.0).astype(BF16)
        attn_s[h] = weights
        mixed_s[:, head(h)] = mm(weights, v_s[:, head(h)], 1, 0)
    chain_finish(0, carried_s)
    for h in range(H):
        mixed_s[:, head(h)] += mm(q_s[:, head(h)], carried_s[h], 1, 0)

    mixed = mixed_s[...]
    scale_rows = jnp.sqrt(jnp.mean(mixed * mixed, axis=-1, keepdims=True) + EPSILON)
    normed = mixed / scale_rows
    nb_s[...] = normed.astype(BF16)
    back = back_s[...]
    dm_s[...] = (
        (back - normed * jnp.mean(back * normed, axis=-1, keepdims=True)) / scale_rows
    ).astype(BF16)
    for h in range(H):
        sown[1, h] = mm(q_s[:, head(h)], dm_s[:, head(h)], 0, 0)
    exchange_start(1)
    bs = []
    for h in range(H):
        scores = mm(dm_s[:, head(h)], v_s[:, head(h)], 1, 1)
        bs.append(jnp.where(causal, scores, 0.0).astype(BF16))
        dqkv_s[0, :, head(h)] = (
            mm(bs[h], k_s[:, head(h)], 1, 0) + mm(dm_s[:, head(h)], carried_s[h], 1, 1)
        ).astype(BF16)
    gather_start(1, dqkv_s[0].astype(F32))
    chain(1)
    columns_start(1, nb_s[...].astype(F32))
    att_ref[...] = mm(nb_s[...], wo[...], 1, 0).astype(BF16)
    for h in range(H):
        mixed_s[:, head(h)] = mm(bs[h], q_s[:, head(h)], 0, 0)
        back_s[:, head(h)] = mm(attn_s[h], dm_s[:, head(h)], 0, 0)
    gather_forward(0)
    columns_finish(0)
    columns_finish(1)
    gather_finish(0)
    partial(0)
    chain_finish(1, later_s)
    for h in range(H):
        dqkv_s[1, :, head(h)] = (
            mixed_s[:, head(h)] + mm(v_s[:, head(h)], later_s[h], 1, 1)
        ).astype(BF16)
    gather_start(2, dqkv_s[1].astype(F32))
    for h in range(H):
        dqkv_s[2, :, head(h)] = (
            back_s[:, head(h)] + mm(k_s[:, head(h)], later_s[h], 1, 0)
        ).astype(BF16)
    gather_start(3, dqkv_s[2].astype(F32))

    gather_forward(1)
    gather_finish(1)
    partial(1)
    pass_on(0)
    dtok = mm(dqkv_s[0], wq[...], 1, 1)
    dtok = dtok + mm(dqkv_s[1], wk[...], 1, 1)
    dtok_ref[...] = (dtok + mm(dqkv_s[2], wv[...], 1, 1)).astype(BF16)
    gather_forward(2)
    gather_finish(2)
    partial(2)
    pass_on(1)
    gather_forward(3)
    gather_finish(3)
    partial(3)
    pass_on(2)
    pass_on(3)
    for k in range(4):
        finish(k)
    for cond, copy in pending:
        if cond is None:
            copy.wait_send()
        else:
            pl.when(cond)(copy.wait_send)
    for k in range(4):
        for zp in range(n_z):
            @pl.when(z != zp)
            def _():
                block_up(k, zp).wait_send()


def local(n_seq, m, tokens, w_query, w_key, w_value, w_output, out_cotangent):
    _, t_rows, width = tokens.shape
    dh = width // H
    n_z, members = n_seq // 2, 2 * m
    rows = width // (n_seq * m)
    vmem, dma = pltpu.VMEM, pltpu.SemaphoreType.DMA
    block = (t_rows, width)
    states = (2, H, dh, dh)
    in_vmem = pl.BlockSpec(memory_space=pltpu.VMEM)
    anywhere = pl.BlockSpec(memory_space=pl.ANY)
    attended, d_tokens, weight_grads = pl.pallas_call(
        functools.partial(kernel, n_seq, m),
        out_shape=(
            jax.ShapeDtypeStruct(block, BF16),
            jax.ShapeDtypeStruct(block, BF16),
            jax.ShapeDtypeStruct((rows, 4 * width), F32),
        ),
        in_specs=[in_vmem, in_vmem] + [anywhere] * 4,
        out_specs=(in_vmem,) * 3,
        scratch_shapes=[vmem((width, width), BF16)] * 4
        + [
            vmem(block, BF16),
            vmem(block, BF16),
            vmem(block, BF16),
            vmem((H, t_rows, t_rows), BF16),
            vmem(block, F32),
            vmem(block, F32),
            vmem((H, dh, dh), BF16),
            vmem((H, dh, dh), BF16),
            vmem(block, BF16),
            vmem(block, BF16),
            vmem((3,) + block, BF16),
            vmem((4, members) + block, F32),
            vmem((2, n_z, 2, m, rows, t_rows), F32),
            vmem((2, members, n_z, rows, t_rows), F32),
            vmem((2, n_z * rows, members * t_rows), BF16),
            vmem((4, n_z, rows, width), F32),
            vmem((4, n_z + 1, rows, width), F32),
            vmem(states, F32),
            vmem(states, F32),
            vmem(states, F32),
            vmem((2, H // 2, dh, dh), F32),
            dma((4,)),
            dma((4, m)),
            dma((4, m)),
            dma((4, members)),
            dma((2, members)),
            dma((2, members)),
            dma((2,)),
            dma((2,)),
            dma((2, H // 2)),
            dma((2, H // 2)),
            dma((2, H // 2)),
            dma((2, H // 2)),
            dma((4, n_z)),
            dma((4, n_z + 1)),
        ],
        compiler_params=pltpu.CompilerParams(
            collective_id=0, has_side_effects=True, vmem_limit_bytes=60 * 2**20
        ),
    )(
        tokens.reshape(block), out_cotangent.reshape(block),
        w_query, w_key, w_value, w_output,
    )
    return attended.reshape(tokens.shape), d_tokens.reshape(tokens.shape), weight_grads


def solution(mesh):
    batch = P(("groups", "dp"), "seq", None)
    return jax.shard_map(
        functools.partial(local, mesh.shape["seq"], mesh.shape["dp"]),
        mesh=mesh,
        in_specs=(batch, P(), P(), P(), P(), batch),
        out_specs=(batch, batch, P(("groups", "seq", "dp"), None)),
        check_vma=False,
    )
```

time: 360 us -> 140 us (0.39)
  waiting for transfers between devices: 249 us -> 0 us
  Pallas kernels: 0 us -> 132 us
  matrix products: 32.2 us -> 0 us
  other arithmetic: 31.3 us -> 0 us
  local copies, waits for them, and re-layouts: 30.9 us -> 5.61 us
  between operations: 14.1 us -> 0.64 us
    unnamed x4 -> x0, waiting for transfers between devices: 170 us -> none
    pallas_call x0 -> x1, Pallas kernels: none -> 132 us  [local(): pl.pallas_call(functools.partial(kernel, n_seq, m), out_shape=(jax.ShapeD...]
    all_gather x2 -> x0, waiting for transfers between devices: 79.1 us -> none  [entering(): everything = lax.all_gather(value, axis)]
    dot_general x22 -> x0, matrix products: 32.2 us -> none  [the longest x3 5.46 us: project(): jnp.dot(flattened, weight, preferred_element_type=jnp.float32)]
    unnamed x52 -> x3, local copies, waits for them, and re-layouts: 28.4 us -> 5.61 us
    select_n x16 -> x0, other arithmetic: 19.7 us -> none  [hop(): return jnp.where(reached, new, before)]
    concatenate x1 -> x0, other arithmetic: 7.14 us -> none  [local(): jnp.concatenate([jnp.einsum('nd,ne->de', flattened, joined, preferred_ele...]
  transfers between devices with their start and end apart: 3 -> 0, of which waited for: 3 -> 0; matrix products, arithmetic and copies ran while one was open for 6% -> 0% of each run, Pallas kernels for 0% -> 0%
where the time goes in v1:
time: 140 us; the launch traced here: 139 us
  Pallas kernels  132 us (94%)
  local copies, waits for them, and re-layouts  5.61 us (4%)
    pallas_call x1, Pallas kernels, local(): pl.pallas_call(functools.partial(kernel, n_seq, m), out_shape=(jax.ShapeD...  132 us
    unnamed x3, local copies, waits for them, and re-layouts  5.61 us

profile of v1, /device:TPU:0, one launch (start us, length us, event | category | flops | bytes accessed | tf_op | source)
XLA Modules:
  0.0 138.6 jit_solution(10736500338259712757)
XLA Ops:
  0.6 132.4 %shard_map.85 = (bf16[128,1024]{1,0:T(8,128)(2,1)}, bf16[128,1024]{1,0:T(8,128)(2,1)}, f32[64,4096]{1,0:T(8,128)}) custom-call(bf16[128,1024]{1,0:T(8,128)(2,1)} %bitcast.4, bf16[128,1024]{1,0:T(8,128)(2,1)} %bitcast.5, bf16[1024,1024]{1,0:T(8,128)(2,1)} %wq_hbm.1, bf16[1024,1024]{1,0:T(8,128)(2,1)} %wk_hbm.1, bf16[1024,1024]{1,0:T(8,128)(2,1)} %wv_hbm.1, ...), custom_call_target="tpu_custom_call" | custom-call | tf_op jit(solution)/shard_map/pallas_call | solution.py:351
  133.0 1.7 %copy.12 = bf16[1,128,1024]{2,1,0:T(8,128)(2,1)} copy(bf16[1,128,1024]{2,1,0:T(8,128)(2,1)} %bitcast.7) | data formatting | bytes 524288
  134.7 1.7 %copy.13 = bf16[1,128,1024]{2,1,0:T(8,128)(2,1)} copy(bf16[1,128,1024]{2,1,0:T(8,128)(2,1)} %bitcast.6) | data formatting | bytes 524288
  136.4 2.3 %copy.14 = f32[64,4096]{1,0:T(8,128)} copy(f32[64,4096]{1,0:T(8,128)} %get-tuple-element.14) | data formatting | bytes 2097152

commit v2 on v1

--- a/solution.py
+++ b/solution.py
@@ -13,6 +13,7 @@
 MESH = pl.DeviceIdType.MESH
 F32, BF16 = jnp.float32, jnp.bfloat16
 COLUMN_BLOCK = (3, 0, 1, 2)
+SPLIT = 2
 
 
 def mm(a, b, ca, cb):
@@ -24,7 +25,7 @@
     tok_ref, cot_ref, wq_hbm, wk_hbm, wv_hbm, wo_hbm,
     att_ref, dtok_ref, wg_ref,
     wq, wk, wv, wo,
-    q_s, k_s, v_s, attn_s, mixed_s, back_s, carried_s, later_s, dm_s, nb_s, dqkv_s,
+    q_s, k_s, v_s, attn_s, bs_s, mixed_s, back_s, carried_s, later_s, dm_s, nb_s, dqkv_s,
     gbuf, xt, xland, lhs, part, inb, sown, spart, crecv, csend,
     w_sem, g_send, g_fwd, g_recv, x_send, x_recv, e_send, e_recv,
     c_send, c_recv, p_send, p_recv, r_send, r_recv,
@@ -42,7 +43,7 @@
     partner = {"seq": 2 * z + 1 - c, "dp": d}
     above = {"seq": jnp.minimum(s + 2, n_seq - 2 + c), "dp": d}
     below = {"seq": jnp.maximum(s - 2, c), "dp": d}
-    pending = []
+    part_width = width // SPLIT
 
     def rcopy(src, dst, ss, rs, dev):
         return pltpu.make_async_remote_copy(
@@ -81,47 +82,52 @@
     def _():
         pl.semaphore_signal(barrier, inc=1, device_id=below, device_id_type=MESH)
 
-    pl.semaphore_wait(
-        barrier, members - 1 + jnp.where(up, 1, 0) + jnp.where(down, 1, 0)
-    )
-
-    def gather_start(k, value):
-        gbuf[k, me] = value
+    def gather_copies(k):
         own = gbuf.at[k, me]
-        first = rcopy(own, own, g_send.at[k, 0], g_recv.at[k, me], partner)
-        first.start()
-        pending.append((None, first))
+        copies = [rcopy(own, own, g_send.at[k, 0], g_recv.at[k, me], partner)]
         for j in range(1, m):
             to = {"seq": s, "dp": lax.rem(d + j, m)}
-            copy = rcopy(own, own, g_send.at[k, j], g_recv.at[k, me], to)
-            copy.start()
-            pending.append((None, copy))
-
-    def gather_forward(k):
+            copies.append(rcopy(own, own, g_send.at[k, j], g_recv.at[k, me], to))
+        return copies
+
+    def forward_copies(k):
+        copies = []
         for j in range(1, m):
             slot = c * m + lax.rem(d + m - j, m)
             ref = gbuf.at[k, slot]
-            arrived(ref, g_recv.at[k, slot])
-            copy = rcopy(ref, ref, g_fwd.at[k, j], g_recv.at[k, slot], partner)
+            copies.append(rcopy(ref, ref, g_fwd.at[k, j], g_recv.at[k, slot], partner))
+        return copies
+
+    def gather_start(matrix, value):
+        for i in range(SPLIT):
+            k = matrix * SPLIT + i
+            gbuf[k, me] = value[:, i * part_width:(i + 1) * part_width].astype(F32)
+            for copy in reversed(gather_copies(k)):
+                copy.start()
+
+    def gather_finish(k):
+        for copy in forward_copies(k):
+            copy.wait_recv()
             copy.start()
-            pending.append((None, copy))
-
-    def gather_finish(k):
         for j in range(m):
             slot = (1 - c) * m + j
             arrived(gbuf.at[k, slot], g_recv.at[k, slot])
 
+    def column_copies(kind):
+        copies = []
+        for rel in range(1, members):
+            t, tc, td = member(rel)
+            copies.append(rcopy(
+                xt.at[kind, :, tc, td], xland.at[kind, me], x_send.at[kind, rel],
+                x_recv.at[kind, me], {"seq": 2 * z + tc, "dp": td},
+            ))
+        return copies
+
     def columns_start(kind, value):
         xt[kind] = value.T.reshape(n_z, 2, m, rows, t_rows)
         xland[kind, me] = xt[kind, :, c, d]
-        for rel in range(1, members):
-            t, tc, td = member(rel)
-            copy = rcopy(
-                xt.at[kind, :, tc, td], xland.at[kind, me], x_send.at[kind, rel],
-                x_recv.at[kind, me], {"seq": 2 * z + tc, "dp": td},
-            )
+        for copy in column_copies(kind):
             copy.start()
-            pending.append((None, copy))
 
     def columns_finish(kind):
         for rel in range(1, members):
@@ -132,13 +138,23 @@
                 xland[kind, j].reshape(n_z * rows, t_rows).astype(BF16)
             )
 
-    def exchange_start(way):
-        copy = rcopy(sown.at[way], spart.at[way], e_send.at[way], e_recv.at[way], partner)
-        copy.start()
-        pending.append((None, copy))
+    def exchange_copy(way):
+        return rcopy(sown.at[way], spart.at[way], e_send.at[way], e_recv.at[way], partner)
+
+    def ends(way):
+        return (down, up, above) if way == 0 else (up, down, below)
+
+    def chain_copies(way, j):
+        h = c * half + j
+        ref = crecv.at[way, h]
+        side = rcopy(ref, ref, p_send.at[way, j], p_recv.at[way, j], partner)
+        ahead = rcopy(
+            csend.at[way, j], ref, c_send.at[way, j], c_recv.at[way, j], ends(way)[2]
+        )
+        return h, side, ahead
 
     def chain(way):
-        has_in, has_out, to = (down, up, above) if way == 0 else (up, down, below)
+        has_in, has_out, _ = ends(way)
         arrived(spart.at[way], e_recv.at[way])
 
         @pl.when(jnp.logical_not(has_in))
@@ -146,14 +162,11 @@
             crecv[way] = jnp.zeros(crecv.shape[1:], F32)
 
         for j in range(half):
-            h = c * half + j
-            ref = crecv.at[way, h]
-            side = rcopy(ref, ref, p_send.at[way, j], p_recv.at[way, j], partner)
-            ahead = rcopy(csend.at[way, j], ref, c_send.at[way, j], c_recv.at[way, j], to)
+            h, side, ahead = chain_copies(way, j)
 
             @pl.when(has_in)
             def _():
-                arrived(ref, c_recv.at[way, j])
+                arrived(crecv.at[way, h], c_recv.at[way, j])
 
             @pl.when(has_out)
             def _():
@@ -164,11 +177,8 @@
             def _():
                 side.start()
 
-            pending.append((has_in, side))
-            pending.append((has_out, ahead))
-
     def chain_finish(way, out):
-        has_in = down if way == 0 else up
+        has_in = ends(way)[0]
         for j in range(half):
             @pl.when(has_in)
             def _():
@@ -191,9 +201,9 @@
         )
 
     def partial(k):
-        right = gbuf[k].reshape(members * t_rows, width).astype(BF16)
-        left = lhs[1 if k == 0 else 0]
-        part[k] = mm(left, right, 1, 0).reshape(n_z, rows, width)
+        right = gbuf[k].reshape(members * t_rows, part_width).astype(BF16)
+        left = lhs[1 if k < SPLIT else 0]
+        part[k] = mm(left, right, 1, 0).reshape(n_z, rows, part_width)
 
         @pl.when(z == 0)
         def _():
@@ -234,8 +244,8 @@
             arrived(inb.at[k, n_z], r_recv.at[k, n_z])
             part[k, z] = part[k, z] + inb[k, n_z]
 
-        at = COLUMN_BLOCK[k] * width
-        wg_ref[:, at:at + width] = part[k, z] * (1.0 / math.sqrt(token_total))
+        at = COLUMN_BLOCK[k // SPLIT] * width + k % SPLIT * part_width
+        wg_ref[:, at:at + part_width] = part[k, z] * (1.0 / math.sqrt(token_total))
 
     def head(h):
         return slice(h * dh, (h + 1) * dh)
@@ -246,11 +256,20 @@
     v_s[...] = mm(tok_ref[...], wv[...], 1, 0).astype(BF16)
     for h in range(H):
         sown[0, h] = mm(k_s[:, head(h)], v_s[:, head(h)], 0, 0)
-    exchange_start(0)
-    gather_start(0, cot_ref[...].astype(F32))
+    pl.semaphore_wait(
+        barrier, members - 1 + jnp.where(up, 1, 0) + jnp.where(down, 1, 0)
+    )
+    exchange_copy(0).start()
+    gather_start(0, cot_ref[...])
     loads[2].wait()
     q_s[...] = mm(tok_ref[...], wq[...], 1, 0).astype(BF16)
-    chain(0)
+    first = z < n_z // 2
+    last = jnp.logical_not(first)
+
+    @pl.when(first)
+    def _():
+        chain(0)
+
     columns_start(0, tok_ref[...].astype(F32))
     loads[3].wait()
     back_s[...] = mm(cot_ref[...], wo[...], 1, 1)
@@ -262,6 +281,11 @@
         weights = jnp.where(causal, scores, 0.0).astype(BF16)
         attn_s[h] = weights
         mixed_s[:, head(h)] = mm(weights, v_s[:, head(h)], 1, 0)
+
+    @pl.when(last)
+    def _():
+        chain(0)
+
     chain_finish(0, carried_s)
     for h in range(H):
         mixed_s[:, head(h)] += mm(q_s[:, head(h)], carried_s[h], 1, 0)
@@ -276,66 +300,128 @@
     ).astype(BF16)
     for h in range(H):
         sown[1, h] = mm(q_s[:, head(h)], dm_s[:, head(h)], 0, 0)
-    exchange_start(1)
-    bs = []
+    exchange_copy(1).start()
+    columns_start(1, nb_s[...].astype(F32))
+
+    @pl.when(last)
+    def _():
+        chain(1)
+
     for h in range(H):
         scores = mm(dm_s[:, head(h)], v_s[:, head(h)], 1, 1)
-        bs.append(jnp.where(causal, scores, 0.0).astype(BF16))
+        bs_s[h] = jnp.where(causal, scores, 0.0).astype(BF16)
         dqkv_s[0, :, head(h)] = (
-            mm(bs[h], k_s[:, head(h)], 1, 0) + mm(dm_s[:, head(h)], carried_s[h], 1, 1)
+            mm(bs_s[h], k_s[:, head(h)], 1, 0) + mm(dm_s[:, head(h)], carried_s[h], 1, 1)
         ).astype(BF16)
-    gather_start(1, dqkv_s[0].astype(F32))
-    chain(1)
-    columns_start(1, nb_s[...].astype(F32))
-    att_ref[...] = mm(nb_s[...], wo[...], 1, 0).astype(BF16)
-    for h in range(H):
-        mixed_s[:, head(h)] = mm(bs[h], q_s[:, head(h)], 0, 0)
+    gather_start(1, dqkv_s[0])
+    for h in range(H):
+        mixed_s[:, head(h)] = mm(bs_s[h], q_s[:, head(h)], 0, 0)
         back_s[:, head(h)] = mm(attn_s[h], dm_s[:, head(h)], 0, 0)
-    gather_forward(0)
-    columns_finish(0)
-    columns_finish(1)
-    gather_finish(0)
-    partial(0)
+
+    def chunks(matrix):
+        return range(matrix * SPLIT, (matrix + 1) * SPLIT)
+
+    def output_chunks():
+        columns_finish(0)
+        columns_finish(1)
+        for k in chunks(0):
+            gather_finish(k)
+            partial(k)
+
+    def query_chunks():
+        for k in chunks(1):
+            gather_finish(k)
+            partial(k)
+
+    @pl.when((z == 0) | last)
+    def _():
+        output_chunks()
+
+    @pl.when(z == 0)
+    def _():
+        query_chunks()
+
+    @pl.when(first)
+    def _():
+        chain(1)
+
     chain_finish(1, later_s)
     for h in range(H):
         dqkv_s[1, :, head(h)] = (
             mixed_s[:, head(h)] + mm(v_s[:, head(h)], later_s[h], 1, 1)
         ).astype(BF16)
-    gather_start(2, dqkv_s[1].astype(F32))
+    gather_start(2, dqkv_s[1])
     for h in range(H):
         dqkv_s[2, :, head(h)] = (
             back_s[:, head(h)] + mm(k_s[:, head(h)], later_s[h], 1, 0)
         ).astype(BF16)
-    gather_start(3, dqkv_s[2].astype(F32))
-
-    gather_forward(1)
-    gather_finish(1)
-    partial(1)
-    pass_on(0)
+    gather_start(3, dqkv_s[2])
+
+    @pl.when((z > 0) & first)
+    def _():
+        output_chunks()
+
+    @pl.when(z > 0)
+    def _():
+        query_chunks()
+
+    for k in chunks(0):
+        pass_on(k)
+    att_ref[...] = mm(nb_s[...], wo[...], 1, 0).astype(BF16)
     dtok = mm(dqkv_s[0], wq[...], 1, 1)
     dtok = dtok + mm(dqkv_s[1], wk[...], 1, 1)
     dtok_ref[...] = (dtok + mm(dqkv_s[2], wv[...], 1, 1)).astype(BF16)
-    gather_forward(2)
-    gather_finish(2)
-    partial(2)
-    pass_on(1)
-    gather_forward(3)
-    gather_finish(3)
-    partial(3)
-    pass_on(2)
-    pass_on(3)
-    for k in range(4):
+    count = 4 * SPLIT
+    for k in range(2 * SPLIT, count):
+        gather_finish(k)
+        partial(k)
+        pass_on(k - SPLIT)
+        finish(k - 2 * SPLIT)
+    for k in range(count - SPLIT, count):
+        pass_on(k)
+        finish(k - SPLIT)
+    for k in range(count - SPLIT, count):
         finish(k)
-    for cond, copy in pending:
-        if cond is None:
+
+    for way in range(2):
+        exchange_copy(way).wait_send()
+        for copy in column_copies(way):
             copy.wait_send()
-        else:
-            pl.when(cond)(copy.wait_send)
-    for k in range(4):
+        has_in, has_out, _ = ends(way)
+        for j in range(half):
+            _, side, ahead = chain_copies(way, j)
+            pl.when(has_in)(side.wait_send)
+            pl.when(has_out)(ahead.wait_send)
+    for k in range(count):
+        for copy in gather_copies(k) + forward_copies(k):
+            copy.wait_send()
         for zp in range(n_z):
             @pl.when(z != zp)
             def _():
                 block_up(k, zp).wait_send()
+
+
+def copy_kernel(count, *refs):
+    sems = refs[-1]
+    copies = [
+        pltpu.make_async_copy(refs[i], refs[count + i], sems.at[i]) for i in range(count)
+    ]
+    for copy in copies:
+        copy.start()
+    for copy in copies:
+        copy.wait()
+
+
+def copied(arrays):
+    count = len(arrays)
+    anywhere = pl.BlockSpec(memory_space=pl.ANY)
+    return pl.pallas_call(
+        functools.partial(copy_kernel, count),
+        out_shape=tuple(jax.ShapeDtypeStruct(a.shape, a.dtype) for a in arrays),
+        in_specs=[anywhere] * count,
+        out_specs=(anywhere,) * count,
+        scratch_shapes=[pltpu.SemaphoreType.DMA((count,))],
+    )(*arrays)
 
 
 def local(n_seq, m, tokens, w_query, w_key, w_value, w_output, out_cotangent):
@@ -343,12 +429,13 @@
     dh = width // H
     n_z, members = n_seq // 2, 2 * m
     rows = width // (n_seq * m)
+    count = 4 * SPLIT
     vmem, dma = pltpu.VMEM, pltpu.SemaphoreType.DMA
     block = (t_rows, width)
     states = (2, H, dh, dh)
     in_vmem = pl.BlockSpec(memory_space=pltpu.VMEM)
     anywhere = pl.BlockSpec(memory_space=pl.ANY)
-    attended, d_tokens, weight_grads = pl.pallas_call(
+    results = pl.pallas_call(
         functools.partial(kernel, n_seq, m),
         out_shape=(
             jax.ShapeDtypeStruct(block, BF16),
@@ -363,6 +450,7 @@
             vmem(block, BF16),
             vmem(block, BF16),
             vmem((H, t_rows, t_rows), BF16),
+            vmem((H, t_rows, t_rows), BF16),
             vmem(block, F32),
             vmem(block, F32),
             vmem((H, dh, dh), BF16),
@@ -370,20 +458,20 @@
             vmem(block, BF16),
             vmem(block, BF16),
             vmem((3,) + block, BF16),
-            vmem((4, members) + block, F32),
+            vmem((count, members, t_rows, width // SPLIT), F32),
             vmem((2, n_z, 2, m, rows, t_rows), F32),
             vmem((2, members, n_z, rows, t_rows), F32),
             vmem((2, n_z * rows, members * t_rows), BF16),
-            vmem((4, n_z, rows, width), F32),
-            vmem((4, n_z + 1, rows, width), F32),
+            vmem((count, n_z, rows, width // SPLIT), F32),
+            vmem((count, n_z + 1, rows, width // SPLIT), F32),
             vmem(states, F32),
             vmem(states, F32),
             vmem(states, F32),
             vmem((2, H // 2, dh, dh), F32),
             dma((4,)),
-            dma((4, m)),
-            dma((4, m)),
-            dma((4, members)),
+            dma((count, m)),
+            dma((count, m)),
+            dma((count, members)),
             dma((2, members)),
             dma((2, members)),
             dma((2,)),
@@ -392,8 +480,8 @@
             dma((2, H // 2)),
             dma((2, H // 2)),
             dma((2, H // 2)),
-            dma((4, n_z)),
-            dma((4, n_z + 1)),
+            dma((count, n_z)),
+            dma((count, n_z + 1)),
         ],
         compiler_params=pltpu.CompilerParams(
             collective_id=0, has_side_effects=True, vmem_limit_bytes=60 * 2**20
@@ -402,6 +490,7 @@
         tokens.reshape(block), out_cotangent.reshape(block),
         w_query, w_key, w_value, w_output,
     )
+    attended, d_tokens, weight_grads = copied(results)
     return attended.reshape(tokens.shape), d_tokens.reshape(tokens.shape), weight_grads
 
 

time: 140 us -> 193 us (1.38)
  Pallas kernels: 132 us -> 192 us
  local copies, waits for them, and re-layouts: 5.61 us -> 0 us
    pallas_call x0 -> x1, Pallas kernels: none -> 48.8 us  [copied(): pl.pallas_call(functools.partial(copy_kernel, count), out_shape=tuple((ja...]
    pallas_call x1, Pallas kernels: 132 us -> 143 us  [local(): pl.pallas_call(functools.partial(kernel, n_seq, m), out_shape=(jax.ShapeD...]
    unnamed x3 -> x0, local copies, waits for them, and re-layouts: 5.61 us -> none
where the time goes in v2:
time: 193 us
  Pallas kernels  192 us (99%)
    pallas_call x1, Pallas kernels, local(): pl.pallas_call(functools.partial(kernel, n_seq, m), out_shape=(jax.ShapeD...  143 us
    pallas_call x1, Pallas kernels, copied(): pl.pallas_call(functools.partial(copy_kernel, count), out_shape=tuple((ja...  48.8 us

profile of v2, /device:TPU:0, one launch (start us, length us, event | category | flops | bytes accessed | tf_op | source)
XLA Modules:
  0.0 192.5 jit_solution(9637276889337838411)
XLA Ops:
  0.6 143.1 %shard_map.85 = (bf16[128,1024]{1,0:T(8,128)(2,1)}, bf16[128,1024]{1,0:T(8,128)(2,1)}, f32[64,4096]{1,0:T(8,128)}) custom-call(bf16[128,1024]{1,0:T(8,128)(2,1)} %bitcast.4, bf16[128,1024]{1,0:T(8,128)(2,1)} %bitcast.5, bf16[1024,1024]{1,0:T(8,128)(2,1)} %wq_hbm.1, bf16[1024,1024]{1,0:T(8,128)(2,1)} %wk_hbm.1, bf16[1024,1024]{1,0:T(8,128)(2,1)} %wv_hbm.1, ...), custom_call_target="tpu_custom_call" | custom-call | tf_op jit(solution)/shard_map/pallas_call | solution.py:438
  143.7 48.8 %shard_map.86 = (bf16[128,1024]{1,0:T(8,128)(2,1)}, bf16[128,1024]{1,0:T(8,128)(2,1)}, f32[64,4096]{1,0:T(8,128)}) custom-call(bf16[128,1024]{1,0:T(8,128)(2,1)} %get-tuple-element.9.refs_0_, bf16[128,1024]{1,0:T(8,128)(2,1)} %get-tuple-element.10.refs_1_, f32[64,4096]{1,0:T(8,128)} %get-tuple-element.11.refs_2_), custom_call_target="tpu_custom_call" | custom-call | tf_op jit(solution)/shard_map/pallas_call | solution.py:418

commit v3 on v2

--- a/solution.py
+++ b/solution.py
@@ -13,7 +13,7 @@
 MESH = pl.DeviceIdType.MESH
 F32, BF16 = jnp.float32, jnp.bfloat16
 COLUMN_BLOCK = (3, 0, 1, 2)
-SPLIT = 2
+SPLIT = 1
 
 
 def mm(a, b, ca, cb):
@@ -263,16 +263,21 @@
     gather_start(0, cot_ref[...])
     loads[2].wait()
     q_s[...] = mm(tok_ref[...], wq[...], 1, 0).astype(BF16)
-    first = z < n_z // 2
-    last = jnp.logical_not(first)
-
-    @pl.when(first)
+    lowest, highest = z == 0, z == n_z - 1
+    middle = (z > 0) & (z < n_z - 1)
+
+    @pl.when(lowest)
     def _():
         chain(0)
 
     columns_start(0, tok_ref[...].astype(F32))
     loads[3].wait()
     back_s[...] = mm(cot_ref[...], wo[...], 1, 1)
+
+    @pl.when(middle)
+    def _():
+        chain(0)
+
     causal = lax.broadcasted_iota(jnp.int32, (t_rows, t_rows), 0) >= (
         lax.broadcasted_iota(jnp.int32, (t_rows, t_rows), 1)
     )
@@ -282,7 +287,7 @@
         attn_s[h] = weights
         mixed_s[:, head(h)] = mm(weights, v_s[:, head(h)], 1, 0)
 
-    @pl.when(last)
+    @pl.when(highest)
     def _():
         chain(0)
 
@@ -303,7 +308,7 @@
     exchange_copy(1).start()
     columns_start(1, nb_s[...].astype(F32))
 
-    @pl.when(last)
+    @pl.when(highest)
     def _():
         chain(1)
 
@@ -314,6 +319,11 @@
             mm(bs_s[h], k_s[:, head(h)], 1, 0) + mm(dm_s[:, head(h)], carried_s[h], 1, 1)
         ).astype(BF16)
     gather_start(1, dqkv_s[0])
+
+    @pl.when(middle)
+    def _():
+        chain(1)
+
     for h in range(H):
         mixed_s[:, head(h)] = mm(bs_s[h], q_s[:, head(h)], 0, 0)
         back_s[:, head(h)] = mm(attn_s[h], dm_s[:, head(h)], 0, 0)
@@ -333,16 +343,11 @@
             gather_finish(k)
             partial(k)
 
-    @pl.when((z == 0) | last)
-    def _():
-        output_chunks()
-
-    @pl.when(z == 0)
+    output_chunks()
+
+    @pl.when(lowest)
     def _():
         query_chunks()
-
-    @pl.when(first)
-    def _():
         chain(1)
 
     chain_finish(1, later_s)
@@ -356,10 +361,6 @@
             back_s[:, head(h)] + mm(k_s[:, head(h)], later_s[h], 1, 0)
         ).astype(BF16)
     gather_start(3, dqkv_s[2])
-
-    @pl.when((z > 0) & first)
-    def _():
-        output_chunks()
 
     @pl.when(z > 0)
     def _():
@@ -402,14 +403,21 @@
 
 
 def copy_kernel(count, *refs):
+    sources, results, held = refs[:count], refs[count:2 * count], refs[2 * count:3 * count]
     sems = refs[-1]
-    copies = [
-        pltpu.make_async_copy(refs[i], refs[count + i], sems.at[i]) for i in range(count)
+    loads = [
+        pltpu.make_async_copy(sources[i], held[i], sems.at[0, i]) for i in range(count)
     ]
-    for copy in copies:
-        copy.start()
-    for copy in copies:
-        copy.wait()
+    stores = [
+        pltpu.make_async_copy(held[i], results[i], sems.at[1, i]) for i in range(count)
+    ]
+    for load in loads:
+        load.start()
+    for load, store in zip(loads, stores):
+        load.wait()
+        store.start()
+    for store in stores:
+        store.wait()
 
 
 def copied(arrays):
@@ -420,7 +428,8 @@
         out_shape=tuple(jax.ShapeDtypeStruct(a.shape, a.dtype) for a in arrays),
         in_specs=[anywhere] * count,
         out_specs=(anywhere,) * count,
-        scratch_shapes=[pltpu.SemaphoreType.DMA((count,))],
+        scratch_shapes=[pltpu.VMEM(a.shape, a.dtype) for a in arrays]
+        + [pltpu.SemaphoreType.DMA((2, count))],
     )(*arrays)
 
 

time: 193 us -> 125 us (0.65)
  Pallas kernels: 192 us -> 124 us
    pallas_call x1, Pallas kernels: 48.8 us -> 2.41 us  [copied(): pl.pallas_call(functools.partial(copy_kernel, count), out_shape=tuple((ja...]
    pallas_call x1, Pallas kernels: 143 us -> 121 us  [local(): pl.pallas_call(functools.partial(kernel, n_seq, m), out_shape=(jax.ShapeD...]
where the time goes in v3:
time: 125 us
  Pallas kernels  124 us (99%)
    pallas_call x1, Pallas kernels, local(): pl.pallas_call(functools.partial(kernel, n_seq, m), out_shape=(jax.ShapeD...  121 us

profile of v3, /device:TPU:0, one launch (start us, length us, event | category | flops | bytes accessed | tf_op | source)
XLA Modules:
  0.0 124.5 jit_solution(18323658303373895798)
XLA Ops:
  0.6 121.5 %shard_map.85 = (bf16[128,1024]{1,0:T(8,128)(2,1)}, bf16[128,1024]{1,0:T(8,128)(2,1)}, f32[64,4096]{1,0:T(8,128)}) custom-call(bf16[128,1024]{1,0:T(8,128)(2,1)} %bitcast.4, bf16[128,1024]{1,0:T(8,128)(2,1)} %bitcast.5, bf16[1024,1024]{1,0:T(8,128)(2,1)} %wq_hbm.1, bf16[1024,1024]{1,0:T(8,128)(2,1)} %wk_hbm.1, bf16[1024,1024]{1,0:T(8,128)(2,1)} %wv_hbm.1, ...), custom_call_target="tpu_custom_call" | custom-call | tf_op jit(solution)/shard_map/pallas_call | solution.py:447
  122.1 2.4 %shard_map.86 = (bf16[128,1024]{1,0:T(8,128)(2,1)}, bf16[128,1024]{1,0:T(8,128)(2,1)}, f32[64,4096]{1,0:T(8,128)}) custom-call(bf16[128,1024]{1,0:T(8,128)(2,1)} %get-tuple-element.9.refs_0_, bf16[128,1024]{1,0:T(8,128)(2,1)} %get-tuple-element.10.refs_1_, f32[64,4096]{1,0:T(8,128)} %get-tuple-element.11.refs_2_), custom_call_target="tpu_custom_call" | custom-call | tf_op jit(solution)/shard_map/pallas_call | solution.py:426

commit v4 on v3

--- a/solution.py
+++ b/solution.py
@@ -14,6 +14,10 @@
 F32, BF16 = jnp.float32, jnp.bfloat16
 COLUMN_BLOCK = (3, 0, 1, 2)
 SPLIT = 1
+
+
+def leads(members):
+    return members <= 8
 
 
 def mm(a, b, ca, cb):
@@ -29,6 +33,7 @@
     gbuf, xt, xland, lhs, part, inb, sown, spart, crecv, csend,
     w_sem, g_send, g_fwd, g_recv, x_send, x_recv, e_send, e_recv,
     c_send, c_recv, p_send, p_recv, r_send, r_recv,
+    top_g, top_x, top_lhs, t_send, t_out, t_fwd, t_recv, tx_send, tx_recv,
 ):
     t_rows, width = tok_ref.shape
     dh = width // H
@@ -40,6 +45,8 @@
     z, c = lax.div(s, 2), lax.rem(s, 2)
     me = c * m + d
     up, down = z < n_z - 1, z > 0
+    lead = leads(members)
+    top, under = (z == n_z - 1) & lead, (z == n_z - 2) & lead
     partner = {"seq": 2 * z + 1 - c, "dp": d}
     above = {"seq": jnp.minimum(s + 2, n_seq - 2 + c), "dp": d}
     below = {"seq": jnp.maximum(s - 2, c), "dp": d}
@@ -74,9 +81,17 @@
             barrier, inc=1, device_id={"seq": 2 * z + tc, "dp": td}, device_id_type=MESH
         )
 
-    @pl.when(up)
+    @pl.when(up & jnp.logical_not(under))
     def _():
         pl.semaphore_signal(barrier, inc=1, device_id=above, device_id_type=MESH)
+
+    @pl.when(under)
+    def _():
+        for t in range(members):
+            pl.semaphore_signal(
+                barrier, inc=1, device_id={"seq": 2 * (z + 1) + t // m, "dp": t % m},
+                device_id_type=MESH,
+            )
 
     @pl.when(down)
     def _():
@@ -138,6 +153,54 @@
                 xland[kind, j].reshape(n_z * rows, t_rows).astype(BF16)
             )
 
+    def top_copies():
+        return [
+            rcopy(gbuf.at[i, me], top_g.at[i, me], t_send.at[i], t_recv.at[i, me], below)
+            for i in range(SPLIT)
+        ]
+
+    def top_gather_copies(i):
+        own = top_g.at[i, me]
+        copies = [rcopy(own, own, t_out.at[i, 0], t_recv.at[i, me], partner)]
+        for j in range(1, m):
+            to = {"seq": s, "dp": lax.rem(d + j, m)}
+            copies.append(rcopy(own, own, t_out.at[i, j], t_recv.at[i, me], to))
+        return copies
+
+    def top_forward_copies(i):
+        copies = []
+        for j in range(1, m):
+            slot = c * m + lax.rem(d + m - j, m)
+            ref = top_g.at[i, slot]
+            copies.append(rcopy(ref, ref, t_fwd.at[i, j], t_recv.at[i, slot], partner))
+        return copies
+
+    def top_column_copies():
+        return [
+            rcopy(
+                xt.at[1, pl.ds(0, n_z - 1), t // m, t % m], top_x.at[me], tx_send.at[t],
+                tx_recv.at[me], {"seq": jnp.maximum(2 * (z - 1), 0) + t // m, "dp": t % m},
+            )
+            for t in range(members)
+        ]
+
+    def top_finish():
+        for t in range(members):
+            arrived(top_x.at[t], tx_recv.at[t])
+            top_lhs[:, t * t_rows:(t + 1) * t_rows] = (
+                top_x[t].reshape((n_z - 1) * rows, t_rows).astype(BF16)
+            )
+        for i in range(SPLIT):
+            for copy in top_forward_copies(i):
+                copy.wait_recv()
+                copy.start()
+            for j in range(m):
+                slot = (1 - c) * m + j
+                arrived(top_g.at[i, slot], t_recv.at[i, slot])
+
+    def highest_of(k):
+        return n_z - 2 if lead and k < SPLIT else n_z - 1
+
     def exchange_copy(way):
         return rcopy(sown.at[way], spart.at[way], e_send.at[way], e_recv.at[way], partner)
 
@@ -205,14 +268,22 @@
         left = lhs[1 if k < SPLIT else 0]
         part[k] = mm(left, right, 1, 0).reshape(n_z, rows, part_width)
 
+        if lead and k < SPLIT:
+            @pl.when(under)
+            def _():
+                extra = top_g[k].reshape(members * t_rows, part_width).astype(BF16)
+                part[k, :n_z - 1] += mm(top_lhs[...], extra, 1, 0).reshape(
+                    n_z - 1, rows, part_width
+                )
+
         @pl.when(z == 0)
         def _():
             for zp in reversed(range(1, n_z)):
                 block_up(k, zp).start()
 
-        @pl.when(z == n_z - 1)
+        @pl.when(z == highest_of(k))
         def _():
-            for zp in range(n_z - 1):
+            for zp in range(highest_of(k)):
                 block_down(k, zp).start()
 
     def pass_on(k):
@@ -225,7 +296,7 @@
                 part[k, high] = part[k, high] + inb[k, high]
                 block_up(k, high).start()
 
-            @pl.when((z < n_z - 1) & (z > low))
+            @pl.when((z < highest_of(k)) & (z > low))
             def _():
                 arrived(inb.at[k, low], r_recv.at[k, low])
                 part[k, low] = part[k, low] + inb[k, low]
@@ -239,7 +310,7 @@
             arrived(inb.at[k, z], r_recv.at[k, z])
             part[k, z] = part[k, z] + inb[k, z]
 
-        @pl.when(up)
+        @pl.when(z < highest_of(k))
         def _():
             arrived(inb.at[k, n_z], r_recv.at[k, n_z])
             part[k, z] = part[k, z] + inb[k, n_z]
@@ -257,10 +328,22 @@
     for h in range(H):
         sown[0, h] = mm(k_s[:, head(h)], v_s[:, head(h)], 0, 0)
     pl.semaphore_wait(
-        barrier, members - 1 + jnp.where(up, 1, 0) + jnp.where(down, 1, 0)
+        barrier, members - 1 + jnp.where(up, 1, 0)
+        + jnp.where(top, members, jnp.where(down, 1, 0))
     )
     exchange_copy(0).start()
     gather_start(0, cot_ref[...])
+
+    def on_lead(condition, action):
+        if lead:
+            pl.when(condition)(action)
+
+    def top_start():
+        for copy in top_copies():
+            copy.start()
+
+    on_lead(top, top_start)
+
     loads[2].wait()
     q_s[...] = mm(tok_ref[...], wq[...], 1, 0).astype(BF16)
     lowest, highest = z == 0, z == n_z - 1
@@ -278,6 +361,8 @@
     def _():
         chain(0)
 
+    columns_finish(0)
+
     causal = lax.broadcasted_iota(jnp.int32, (t_rows, t_rows), 0) >= (
         lax.broadcasted_iota(jnp.int32, (t_rows, t_rows), 1)
     )
@@ -291,6 +376,13 @@
     def _():
         chain(0)
 
+    def top_spread():
+        for i in range(SPLIT):
+            arrived(top_g.at[i, me], t_recv.at[i, me])
+            for copy in reversed(top_gather_copies(i)):
+                copy.start()
+
+    on_lead(under, top_spread)
     chain_finish(0, carried_s)
     for h in range(H):
         mixed_s[:, head(h)] += mm(q_s[:, head(h)], carried_s[h], 1, 0)
@@ -311,6 +403,9 @@
     @pl.when(highest)
     def _():
         chain(1)
+        if lead:
+            for copy in top_column_copies():
+                copy.start()
 
     for h in range(H):
         scores = mm(dm_s[:, head(h)], v_s[:, head(h)], 1, 1)
@@ -324,16 +419,12 @@
     def _():
         chain(1)
 
-    for h in range(H):
-        mixed_s[:, head(h)] = mm(bs_s[h], q_s[:, head(h)], 0, 0)
-        back_s[:, head(h)] = mm(attn_s[h], dm_s[:, head(h)], 0, 0)
-
     def chunks(matrix):
         return range(matrix * SPLIT, (matrix + 1) * SPLIT)
 
     def output_chunks():
-        columns_finish(0)
         columns_finish(1)
+        on_lead(under, top_finish)
         for k in chunks(0):
             gather_finish(k)
             partial(k)
@@ -344,6 +435,9 @@
             partial(k)
 
     output_chunks()
+    for h in range(H):
+        mixed_s[:, head(h)] = mm(bs_s[h], q_s[:, head(h)], 0, 0)
+        back_s[:, head(h)] = mm(attn_s[h], dm_s[:, head(h)], 0, 0)
 
     @pl.when(lowest)
     def _():
@@ -384,6 +478,18 @@
     for k in range(count - SPLIT, count):
         finish(k)
 
+    def top_sent():
+        for copy in top_copies() + top_column_copies():
+            copy.wait_send()
+
+    def under_sent():
+        for i in range(SPLIT):
+            for copy in top_gather_copies(i) + top_forward_copies(i):
+                copy.wait_send()
+
+    on_lead(top, top_sent)
+    on_lead(under, under_sent)
+
     for way in range(2):
         exchange_copy(way).wait_send()
         for copy in column_copies(way):
@@ -397,7 +503,7 @@
         for copy in gather_copies(k) + forward_copies(k):
             copy.wait_send()
         for zp in range(n_z):
-            @pl.when(z != zp)
+            @pl.when((z < zp) | ((z > zp) & (z <= highest_of(k))))
             def _():
                 block_up(k, zp).wait_send()
 
@@ -439,6 +545,7 @@
     n_z, members = n_seq // 2, 2 * m
     rows = width // (n_seq * m)
     count = 4 * SPLIT
+    top_members = members if leads(members) else 1
     vmem, dma = pltpu.VMEM, pltpu.SemaphoreType.DMA
     block = (t_rows, width)
     states = (2, H, dh, dh)
@@ -491,6 +598,15 @@
             dma((2, H // 2)),
             dma((count, n_z)),
             dma((count, n_z + 1)),
+            vmem((SPLIT, top_members, t_rows, width // SPLIT), F32),
+            vmem((top_members, n_z - 1, rows, t_rows), F32),
+            vmem(((n_z - 1) * rows, top_members * t_rows), BF16),
+            dma((SPLIT,)),
+            dma((SPLIT, m)),
+            dma((SPLIT, m)),
+            dma((SPLIT, members)),
+            dma((members,)),
+            dma((members,)),
         ],
         compiler_params=pltpu.CompilerParams(
             collective_id=0, has_side_effects=True, vmem_limit_bytes=60 * 2**20

time: 125 us -> 130 us (1.040)
  Pallas kernels: 124 us -> 130 us
    pallas_call x1, Pallas kernels: 121 us -> 127 us  [local(): pl.pallas_call(functools.partial(kernel, n_seq, m), out_shape=(jax.ShapeD...]
where the time goes in v4:
time: 130 us
  Pallas kernels  130 us (100%)
    pallas_call x1, Pallas kernels, local(): pl.pallas_call(functools.partial(kernel, n_seq, m), out_shape=(jax.ShapeD...  127 us

profile of v4, /device:TPU:0, one launch (start us, length us, event | category | flops | bytes accessed | tf_op | source)
XLA Modules:
  0.0 130.1 jit_solution(12258505864204944012)
XLA Ops:
  0.6 127.1 %shard_map.85 = (bf16[128,1024]{1,0:T(8,128)(2,1)}, bf16[128,1024]{1,0:T(8,128)(2,1)}, f32[64,4096]{1,0:T(8,128)}) custom-call(bf16[128,1024]{1,0:T(8,128)(2,1)} %bitcast.4, bf16[128,1024]{1,0:T(8,128)(2,1)} %bitcast.5, bf16[1024,1024]{1,0:T(8,128)(2,1)} %wq_hbm.1, bf16[1024,1024]{1,0:T(8,128)(2,1)} %wk_hbm.1, bf16[1024,1024]{1,0:T(8,128)(2,1)} %wv_hbm.1, ...), custom_call_target="tpu_custom_call" | custom-call | tf_op jit(solution)/shard_map/pallas_call | solution.py:554
  127.7 2.4 %shard_map.86 = (bf16[128,1024]{1,0:T(8,128)(2,1)}, bf16[128,1024]{1,0:T(8,128)(2,1)}, f32[64,4096]{1,0:T(8,128)}) custom-call(bf16[128,1024]{1,0:T(8,128)(2,1)} %get-tuple-element.9.refs_0_, bf16[128,1024]{1,0:T(8,128)(2,1)} %get-tuple-element.10.refs_1_, f32[64,4096]{1,0:T(8,128)} %get-tuple-element.11.refs_2_), custom_call_target="tpu_custom_call" | custom-call | tf_op jit(solution)/shard_map/pallas_call | solution.py:532

commit v5 on v3

--- a/solution.py
+++ b/solution.py
@@ -319,14 +319,13 @@
             mm(bs_s[h], k_s[:, head(h)], 1, 0) + mm(dm_s[:, head(h)], carried_s[h], 1, 1)
         ).astype(BF16)
     gather_start(1, dqkv_s[0])
-
-    @pl.when(middle)
-    def _():
-        chain(1)
-
     for h in range(H):
         mixed_s[:, head(h)] = mm(bs_s[h], q_s[:, head(h)], 0, 0)
         back_s[:, head(h)] = mm(attn_s[h], dm_s[:, head(h)], 0, 0)
+
+    @pl.when(middle)
+    def _():
+        chain(1)
 
     def chunks(matrix):
         return range(matrix * SPLIT, (matrix + 1) * SPLIT)
@@ -343,7 +342,9 @@
             gather_finish(k)
             partial(k)
 
-    output_chunks()
+    @pl.when(jnp.logical_not(middle))
+    def _():
+        output_chunks()
 
     @pl.when(lowest)
     def _():
@@ -361,6 +362,10 @@
             back_s[:, head(h)] + mm(k_s[:, head(h)], later_s[h], 1, 0)
         ).astype(BF16)
     gather_start(3, dqkv_s[2])
+
+    @pl.when(middle)
+    def _():
+        output_chunks()
 
     @pl.when(z > 0)
     def _():

time: 125 us -> 125 us (level)
  no operation moved by 1% of the time
where the time goes in v5:
time: 125 us
  Pallas kernels  124 us (99%)
    pallas_call x1, Pallas kernels, local(): pl.pallas_call(functools.partial(kernel, n_seq, m), out_shape=(jax.ShapeD...  121 us

profile of v5, /device:TPU:0, one launch (start us, length us, event | category | flops | bytes accessed | tf_op | source)
XLA Modules:
  0.0 124.5 jit_solution(11996547257962500959)
XLA Ops:
  0.6 121.5 %shard_map.85 = (bf16[128,1024]{1,0:T(8,128)(2,1)}, bf16[128,1024]{1,0:T(8,128)(2,1)}, f32[64,4096]{1,0:T(8,128)}) custom-call(bf16[128,1024]{1,0:T(8,128)(2,1)} %bitcast.4, bf16[128,1024]{1,0:T(8,128)(2,1)} %bitcast.5, bf16[1024,1024]{1,0:T(8,128)(2,1)} %wq_hbm.1, bf16[1024,1024]{1,0:T(8,128)(2,1)} %wk_hbm.1, bf16[1024,1024]{1,0:T(8,128)(2,1)} %wv_hbm.1, ...), custom_call_target="tpu_custom_call" | custom-call | tf_op jit(solution)/shard_map/pallas_call | solution.py:452
  122.1 2.4 %shard_map.86 = (bf16[128,1024]{1,0:T(8,128)(2,1)}, bf16[128,1024]{1,0:T(8,128)(2,1)}, f32[64,4096]{1,0:T(8,128)}) custom-call(bf16[128,1024]{1,0:T(8,128)(2,1)} %get-tuple-element.9.refs_0_, bf16[128,1024]{1,0:T(8,128)(2,1)} %get-tuple-element.10.refs_1_, f32[64,4096]{1,0:T(8,128)} %get-tuple-element.11.refs_2_), custom_call_target="tpu_custom_call" | custom-call | tf_op jit(solution)/shard_map/pallas_call | solution.py:431

commit v6 on v5

--- a/solution.py
+++ b/solution.py
@@ -13,7 +13,7 @@
 MESH = pl.DeviceIdType.MESH
 F32, BF16 = jnp.float32, jnp.bfloat16
 COLUMN_BLOCK = (3, 0, 1, 2)
-SPLIT = 1
+SPLIT = 2
 
 
 def mm(a, b, ca, cb):

time: 125 us -> 147 us (1.18)
  Pallas kernels: 124 us -> 146 us
    pallas_call x1, Pallas kernels: 121 us -> 143 us  [local(): pl.pallas_call(functools.partial(kernel, n_seq, m), out_shape=(jax.ShapeD...]
where the time goes in v6:
time: 147 us; the launch traced here: 146 us
  Pallas kernels  146 us (99%)
    pallas_call x1, Pallas kernels, local(): pl.pallas_call(functools.partial(kernel, n_seq, m), out_shape=(jax.ShapeD...  143 us

profile of v6, /device:TPU:0, one launch (start us, length us, event | category | flops | bytes accessed | tf_op | source)
XLA Modules:
  0.0 146.4 jit_solution(9703973114711395748)
XLA Ops:
  0.6 143.3 %shard_map.85 = (bf16[128,1024]{1,0:T(8,128)(2,1)}, bf16[128,1024]{1,0:T(8,128)(2,1)}, f32[64,4096]{1,0:T(8,128)}) custom-call(bf16[128,1024]{1,0:T(8,128)(2,1)} %bitcast.4, bf16[128,1024]{1,0:T(8,128)(2,1)} %bitcast.5, bf16[1024,1024]{1,0:T(8,128)(2,1)} %wq_hbm.1, bf16[1024,1024]{1,0:T(8,128)(2,1)} %wk_hbm.1, bf16[1024,1024]{1,0:T(8,128)(2,1)} %wv_hbm.1, ...), custom_call_target="tpu_custom_call" | custom-call | tf_op jit(solution)/shard_map/pallas_call | solution.py:452
  144.0 2.4 %shard_map.86 = (bf16[128,1024]{1,0:T(8,128)(2,1)}, bf16[128,1024]{1,0:T(8,128)(2,1)}, f32[64,4096]{1,0:T(8,128)}) custom-call(bf16[128,1024]{1,0:T(8,128)(2,1)} %get-tuple-element.9.refs_0_, bf16[128,1024]{1,0:T(8,128)(2,1)} %get-tuple-element.10.refs_1_, f32[64,4096]{1,0:T(8,128)} %get-tuple-element.11.refs_2_), custom_call_target="tpu_custom_call" | custom-call | tf_op jit(solution)/shard_map/pallas_call | solution.py:431

commit v7 on v5

--- a/solution.py
+++ b/solution.py
@@ -215,21 +215,38 @@
             for zp in range(n_z - 1):
                 block_down(k, zp).start()
 
-    def pass_on(k):
-        for step in range(n_z - 1):
-            high, low = n_z - 1 - step, step
-
+    def pass_up(k):
+        for high in reversed(range(1, n_z)):
             @pl.when((z > 0) & (z < high))
             def _():
                 arrived(inb.at[k, high], r_recv.at[k, high])
                 part[k, high] = part[k, high] + inb[k, high]
                 block_up(k, high).start()
 
+    def pass_down(k):
+        for low in range(n_z - 1):
             @pl.when((z < n_z - 1) & (z > low))
             def _():
                 arrived(inb.at[k, low], r_recv.at[k, low])
                 part[k, low] = part[k, low] + inb[k, low]
                 block_down(k, low).start()
+
+    lower = z < n_z // 2
+
+    def pass_on(near, far):
+        @pl.when(lower)
+        def _():
+            if near is not None:
+                pass_up(near)
+            if far is not None:
+                pass_down(far)
+
+        @pl.when(jnp.logical_not(lower))
+        def _():
+            if near is not None:
+                pass_down(near)
+            if far is not None:
+                pass_up(far)
 
     token_total = t_rows * n_seq * m
 
@@ -367,26 +384,26 @@
     def _():
         output_chunks()
 
+    pass_on(0, None)
+
     @pl.when(z > 0)
     def _():
         query_chunks()
 
-    for k in chunks(0):
-        pass_on(k)
-    att_ref[...] = mm(nb_s[...], wo[...], 1, 0).astype(BF16)
+    pass_on(1, 0)
     dtok = mm(dqkv_s[0], wq[...], 1, 1)
     dtok = dtok + mm(dqkv_s[1], wk[...], 1, 1)
     dtok_ref[...] = (dtok + mm(dqkv_s[2], wv[...], 1, 1)).astype(BF16)
+    gather_finish(2)
+    partial(2)
+    pass_on(2, 1)
+    att_ref[...] = mm(nb_s[...], wo[...], 1, 0).astype(BF16)
+    gather_finish(3)
+    partial(3)
+    pass_on(3, 2)
+    pass_on(None, 3)
     count = 4 * SPLIT
-    for k in range(2 * SPLIT, count):
-        gather_finish(k)
-        partial(k)
-        pass_on(k - SPLIT)
-        finish(k - 2 * SPLIT)
-    for k in range(count - SPLIT, count):
-        pass_on(k)
-        finish(k - SPLIT)
-    for k in range(count - SPLIT, count):
+    for k in range(count):
         finish(k)
 
     for way in range(2):

time: 125 us -> 114 us (0.912)
  Pallas kernels: 124 us -> 113 us
    pallas_call x1, Pallas kernels: 121 us -> 110 us  [local(): pl.pallas_call(functools.partial(kernel, n_seq, m), out_shape=(jax.ShapeD...]
where the time goes in v7:
time: 114 us
  Pallas kernels  113 us (99%)
    pallas_call x1, Pallas kernels, local(): pl.pallas_call(functools.partial(kernel, n_seq, m), out_shape=(jax.ShapeD...  110 us
    pallas_call x1, Pallas kernels, copied(): pl.pallas_call(functools.partial(copy_kernel, count), out_shape=tuple((ja...  2.41 us

profile of v7, /device:TPU:0, one launch (start us, length us, event | category | flops | bytes accessed | tf_op | source)
XLA Modules:
  0.0 113.5 jit_solution(6689077892837224051)
XLA Ops:
  0.6 110.5 %shard_map.85 = (bf16[128,1024]{1,0:T(8,128)(2,1)}, bf16[128,1024]{1,0:T(8,128)(2,1)}, f32[64,4096]{1,0:T(8,128)}) custom-call(bf16[128,1024]{1,0:T(8,128)(2,1)} %bitcast.4, bf16[128,1024]{1,0:T(8,128)(2,1)} %bitcast.5, bf16[1024,1024]{1,0:T(8,128)(2,1)} %wq_hbm.1, bf16[1024,1024]{1,0:T(8,128)(2,1)} %wk_hbm.1, bf16[1024,1024]{1,0:T(8,128)(2,1)} %wv_hbm.1, ...), custom_call_target="tpu_custom_call" | custom-call | tf_op jit(solution)/shard_map/pallas_call | solution.py:469
  111.1 2.4 %shard_map.86 = (bf16[128,1024]{1,0:T(8,128)(2,1)}, bf16[128,1024]{1,0:T(8,128)(2,1)}, f32[64,4096]{1,0:T(8,128)}) custom-call(bf16[128,1024]{1,0:T(8,128)(2,1)} %get-tuple-element.9.refs_0_, bf16[128,1024]{1,0:T(8,128)(2,1)} %get-tuple-element.10.refs_1_, f32[64,4096]{1,0:T(8,128)} %get-tuple-element.11.refs_2_), custom_call_target="tpu_custom_call" | custom-call | tf_op jit(solution)/shard_map/pallas_call | solution.py:448
